TPU v7x, 32 devices: a whole 2x2x4 slice. The times are simulated.
32 devices in a mesh: ctx: 4 (over x, core), row: 4 (over z), col: 2 (over y).
Axes of the slice: x: 2, y: 2, z: 4, core: 2. Of those that a mesh axis runs over, the one named last changes fastest.
Arguments:
- states: bfloat16 [384, 4096], P('ctx', 'row'), may hold values from -6 to 6
- context: bfloat16 [384, 4096], P('ctx', 'row'), may hold values from -6 to 6
- up_weight: bfloat16 [4096, 8192], P('row', 'col'), may hold values from -0.09375 to 0.09375
- down_weight: bfloat16 [8192, 4096], P('col', 'row'), may hold values from -0.0625 to 0.0625
- cotangent: bfloat16 [384, 4096], P('ctx', 'row'), may hold values from -6 to 6
Outputs:
- latent: bfloat16 [384, 4096], P('ctx', 'row')
- logdet: float32 [384], P(('ctx', 'row'))
- grad_states: bfloat16 [384, 4096], P('ctx', 'row')
- grad_context: bfloat16 [384, 4096], P('ctx', 'row')
- grad_up: float32 [4096, 8192], P('row', 'col')
- grad_down: float32 [8192, 4096], P('col', 'row')
All inputs are finite; a program needn't handle non-finite values.
Results may differ from a plain program's by a relative error of at most 0.024.
Values may be sent and summed in bfloat16 or wider, within the bound.
A program may use at most 192 MiB of HBM per device.

v0:
```python
import jax
import jax.numpy as jnp
from jax import lax
from jax.sharding import PartitionSpec as P


def silu_slope(hidden):
    sigmoid_part = jax.nn.sigmoid(hidden)
    return sigmoid_part * (1.0 + hidden * (1.0 - sigmoid_part))


def collect(row_block):
    return lax.all_gather(row_block, "row", axis=0, tiled=True)


def feature_total(partial_terms):
    return lax.psum(partial_terms.astype(jnp.bfloat16), "col").astype(jnp.float32)


def contract(left_side, right_side, left_dim, right_dim):
    return lax.dot_general(
        left_side,
        right_side,
        (((left_dim,), (right_dim,)), ((), ())),
        preferred_element_type=jnp.float32,
    )


def shards(states, context, up_weight, down_weight, cotangent):
    hidden = lax.psum_scatter(
        jnp.dot(context, up_weight, preferred_element_type=jnp.float32).astype(jnp.bfloat16),
        "row",
        scatter_dimension=0,
        tiled=True,
    ).astype(jnp.float32)
    activations = collect(jax.nn.silu(hidden).astype(jnp.bfloat16))
    output_terms = jnp.dot(activations, down_weight, preferred_element_type=jnp.float32)
    mixed_total = feature_total(output_terms)
    log_scale = jnp.tanh(mixed_total)
    shrink = jnp.exp(-log_scale)
    flowed = states.astype(jnp.float32) * shrink
    cotangent_wide = cotangent.astype(jnp.float32)
    det_terms = -jnp.sum(log_scale, axis=1)
    scale_rows = ((1.0 - cotangent_wide * flowed) * (1.0 - log_scale * log_scale)).astype(
        jnp.bfloat16
    )
    down_part = contract(activations, scale_rows, 0, 0)
    grad_down = lax.psum(down_part.astype(jnp.bfloat16), "ctx").astype(jnp.float32)
    back_terms = contract(scale_rows, down_weight, 1, 1)
    back_rows = lax.psum_scatter(
        back_terms.astype(jnp.bfloat16), "row", scatter_dimension=0, tiled=True
    ).astype(jnp.float32)
    logdet = lax.psum_scatter(det_terms, "row", scatter_dimension=0, tiled=True)
    slope_rows = (back_rows * silu_slope(hidden)).astype(jnp.bfloat16)
    slope_all = collect(slope_rows)
    input_terms = contract(slope_all, up_weight, 1, 1)
    grad_states = (cotangent_wide * shrink).astype(jnp.bfloat16)
    grad_context = feature_total(input_terms).astype(jnp.bfloat16)
    up_part = contract(context, slope_all, 0, 0)
    grad_up = lax.psum(up_part.astype(jnp.bfloat16), "ctx").astype(jnp.float32)
    return (flowed.astype(jnp.bfloat16), logdet, grad_states, grad_context, grad_up, grad_down)


def solution(mesh):
    placed = (P("ctx", "row"), P("ctx", "row"), P("row", "col"), P("col", "row"), P("ctx", "row"))
    return jax.shard_map(
        shards,
        mesh=mesh,
        in_specs=placed,
        out_specs=(
            P("ctx", "row"),
            P(("ctx", "row")),
            P("ctx", "row"),
            P("ctx", "row"),
            P("row", "col"),
            P("col", "row"),
        ),
        check_vma=False,
    )
```

profile of v0, /device:TPU:0, one launch (start us, length us, event | category | flops | bytes accessed | tf_op | source)
XLA Modules:
  0.0 463.3 jit_solution(15541179772895529971)
XLA Ops:
  7.2 0.9 copy-done
  8.1 5.7 %convolution_convert_fusion.2 = bf16[96,4096]{1,0:T(8,128)(2,1)} fusion(bf16[96,1024]{1,0:T(8,128)(2,1)S(1)} %copy-done, bf16[1024,4096]{1,0:T(8,128)(2,1)} %param.7), kind=kOutput, calls=%fused_computation.3 | convolution fusion | flops 805699584 | bytes 9371648 | tf_op jit(solution)/shard_map/dot_general | solution.py:31
  13.9 26.1 %reduce-scatter.3.cloned.1.call-done = bf16[24,4096]{1,0:T(8,128)(2,1)} async-done(((bf16[96,4096]{1,0:T(8,128)(2,1)}), bf16[24,4096]{1,0:T(8,128)(2,1)}) %reduce-scatter.3.cloned.1.call-update) | async-done | bytes 196624 | tf_op jit(solution)/shard_map/reduce_scatter | solution.py:30
  40.0 1.0 fusion.7
  41.0 18.0 %all_gather.6 = bf16[96,4096]{1,0:T(8,128)(2,1)S(1)} all-gather(bf16[24,4096]{1,0:T(8,128)(2,1)S(1)} %fusion.7), channel_id=1, replica_groups=mesh['ctx'=4,'row'=4,'col'=2] {'row'}, dimensions={0}, use_global_device_ids=true | all-gather | bytes 983040 | tf_op jit(solution)/shard_map/all_gather | solution.py:13
  59.0 5.6 %convolution_convert_fusion.4 = bf16[96,1024]{1,0:T(8,128)(2,1)} fusion(bf16[96,4096]{1,0:T(8,128)(2,1)S(1)} %all_gather.6, bf16[4096,1024]{1,0:T(8,128)(2,1)} %param.8), kind=kOutput, calls=%fused_computation.5 | convolution fusion | flops 805404672 | bytes 9371648 | tf_op jit(solution)/shard_map/dot_general | solution.py:37
  64.7 21.7 %all-reduce.6.cloned.1.call-done = bf16[96,1024]{1,0:T(8,128)(2,1)} async-done(((bf16[96,1024]{1,0:T(8,128)(2,1)}), bf16[96,1024]{1,0:T(8,128)(2,1)}) %all-reduce.6.cloned.1.call-update) | async-done | bytes 196624 | tf_op jit(solution)/shard_map/psum | solution.py:17
  86.4 7.1 %convolution_convert_fusion.1 = bf16[96,4096]{1,0:T(8,128)(2,1)} fusion(bf16[4096,1024]{1,0:T(8,128)(2,1)} %param.8, bf16[96,1024]{1,0:T(8,128)(2,1)S(1)} %copy-done.2, bf16[96,1024]{1,0:T(8,128)(2,1)} %all-reduce.6.cloned.1.call-done, bf16[96,1024]{1,0:T(8,128)(2,1)S(1)} %copy-done.3), kind=kOutput, calls=%fused_computation.2 | convolution fusion | flops 806780928 | bytes 9764864 | tf_op jit(solution)/shard_map/dot_general | solution.py:21
  93.6 5.8 %convolution_convert_fusion = bf16[4096,1024]{1,0:T(8,128)(2,1)} fusion(bf16[96,4096]{1,0:T(8,128)(2,1)S(1)} %all_gather.6, bf16[96,1024]{1,0:T(8,128)(2,1)S(1)} %copy-done.2, bf16[96,1024]{1,0:T(8,128)(2,1)S(1)} %copy-done.4, bf16[96,1024]{1,0:T(8,128)(2,1)S(1)} %copy-done.3), kind=kOutput, calls=%fused_computation.1 | convolution fusion | flops 810582016 | bytes 9764864 | tf_op jit(solution)/shard_map/dot_general | solution.py:21
  99.4 17.6 %reduce-scatter.5.cloned.1.call-done = bf16[24,4096]{1,0:T(8,128)(2,1)} async-done(((bf16[96,4096]{1,0:T(8,128)(2,1)}), bf16[24,4096]{1,0:T(8,128)(2,1)}) %reduce-scatter.5.cloned.1.call-update) | async-done | bytes 196624 | tf_op jit(solution)/shard_map/reduce_scatter | solution.py:50
  117.0 1.1 fusion.11
  118.1 17.9 %all_gather.7 = bf16[96,4096]{1,0:T(8,128)(2,1)S(1)} all-gather(bf16[24,4096]{1,0:T(8,128)(2,1)S(1)} %fusion.11), channel_id=1, replica_groups=mesh['ctx'=4,'row'=4,'col'=2] {'row'}, dimensions={0}, use_global_device_ids=true | all-gather | bytes 983040 | tf_op jit(solution)/shard_map/all_gather | solution.py:13
  136.1 5.8 %convert_bitcast_fusion = bf16[1024,4096]{0,1:T(8,128)(2,1)} fusion(bf16[96,4096]{1,0:T(8,128)(2,1)S(1)} %all_gather.7, bf16[96,1024]{1,0:T(8,128)(2,1)S(1)} %copy-done), kind=kOutput, calls=%fused_computation | convolution fusion | flops 809500672 | bytes 9371648 | tf_op jit(solution)/shard_map/dot_general | solution.py:21
  142.1 0.4 copy-done.6
  142.5 0.6 dynamic-slice
  143.7 7.2 %convolution_convert_fusion.3 = bf16[96,1024]{1,0:T(8,128)(2,1)} fusion(bf16[96,4096]{1,0:T(8,128)(2,1)S(1)} %all_gather.7, bf16[1024,4096]{1,0:T(8,128)(2,1)} %param.7), kind=kOutput, calls=%fused_computation.4 | convolution fusion | flops 805404672 | bytes 9371648 | tf_op jit(solution)/shard_map/dot_general | solution.py:21
  151.0 1.0 fusion
  152.0 9.6 %all-reduce = f32[96]{0:T(128)S(1)} all-reduce(f32[96]{0:T(128)S(1)} %neg.13), channel_id=3, replica_groups=mesh['ctx'=4,'row'=4,'col'=2] {'row'}, use_global_device_ids=true, to_apply=%region_3.4.clone | all-reduce | flops 96 | bytes 768
  161.6 0.6 dynamic-slice.1
  162.2 268.0 %all-reduce.10.cloned.1.call-done = (bf16[1024,4096]{0,1:T(8,128)(2,1)}, bf16[4096,1024]{1,0:T(8,128)(2,1)}) async-done(((bf16[1024,4096]{0,1:T(8,128)(2,1)}, bf16[4096,1024]{1,0:T(8,128)(2,1)}), (bf16[1024,4096]{0,1:T(8,128)(2,1)}, bf16[4096,1024]{1,0:T(8,128)(2,1)})) %all-reduce.10.cloned.1.call-update) | async-done | bytes 16777232 | tf_op jit(solution)/shard_map/psum | solution.py:60
  430.1 12.3 %copy.12 = f32[1024,4096]{1,0:T(8,128)} copy(bf16[1024,4096]{0,1:T(8,128)(2,1)} %get-tuple-element.18) | data formatting | bytes 25165824
  442.5 11.8 %convert_element_type.77 = f32[4096,1024]{1,0:T(8,128)} convert(bf16[4096,1024]{1,0:T(8,128)(2,1)} %get-tuple-element.19) | non-fusion elementwise | flops 4194304 | bytes 25165824 | tf_op jit(solution)/shard_map/convert_element_type | solution.py:48
  454.2 1.0 all-reduce.8.cloned.1.call-done
  455.2 1.6 copy.17
  (23 shorter events, 0.5 us)
Async XLA Ops:
  7.2 0.9 copy-start
  7.2 32.8 %reduce-scatter.3.cloned.1.call-start = ((), (), s32[]{:S(2)}) async-start(), calls=%async_computation.2 | async-start | bytes 983040 | tf_op jit(solution)/shard_map/reduce_scatter | solution.py:30
  13.8 72.5 %all-reduce.6.cloned.1.call-start = ((), (), s32[]{:S(2)}) async-start(), calls=%async_computation.3 | async-start | bytes 393216 | tf_op jit(solution)/shard_map/psum | solution.py:17
  59.0 27.3 %copy-start.2 = (bf16[96,1024]{1,0:T(8,128)(2,1)S(1)}, bf16[96,1024]{1,0:T(8,128)(2,1)}, u32[]{:S(2)}) copy-start(bf16[96,1024]{1,0:T(8,128)(2,1)} %param.9) | copy-start | bytes 589828
  59.0 27.3 %copy-start.3 = (bf16[96,1024]{1,0:T(8,128)(2,1)S(1)}, bf16[96,1024]{1,0:T(8,128)(2,1)}, u32[]{:S(2)}) copy-start(bf16[96,1024]{1,0:T(8,128)(2,1)} %param.5) | copy-start | bytes 589828
  64.6 52.4 %reduce-scatter.5.cloned.1.call-start = ((), (), s32[]{:S(2)}) async-start(), calls=%async_computation.4 | async-start | bytes 983040 | tf_op jit(solution)/shard_map/reduce_scatter | solution.py:50
  86.4 7.2 %copy-start.4 = (bf16[96,1024]{1,0:T(8,128)(2,1)S(1)}, bf16[96,1024]{1,0:T(8,128)(2,1)}, u32[]{:S(2)}) copy-start(bf16[96,1024]{1,0:T(8,128)(2,1)} %all-reduce.6.cloned.1.call-done) | copy-start | bytes 589828
  93.5 23.5 %copy-start.5 = (bf16[24,4096]{1,0:T(8,128)(2,1)S(1)}, bf16[24,4096]{1,0:T(8,128)(2,1)}, u32[]{:S(2)}) copy-start(bf16[24,4096]{1,0:T(8,128)(2,1)} %reduce-scatter.3.cloned.1.call-done) | copy-start | bytes 589828
  93.5 336.6 %all-reduce.10.cloned.1.call-start = ((), (), s32[]{:S(2)}) async-start(), calls=%async_computation.6 | async-start | bytes 33554432 | tf_op jit(solution)/shard_map/psum | solution.py:60
  141.8 0.7 copy-start.6
  141.9 313.3 %all-reduce.8.cloned.1.call-start = ((), (), s32[]{:S(2)}) async-start(), calls=%async_computation.5 | async-start | bytes 393216 | tf_op jit(solution)/shard_map/psum | solution.py:17
  442.5 14.3 %copy-start.1 = (bf16[96,1024]{1,0:T(8,128)(2,1)S(1)}, bf16[96,1024]{1,0:T(8,128)(2,1)}, u32[]{:S(2)}) copy-start(bf16[96,1024]{1,0:T(8,128)(2,1)} %param.6) | copy-start | bytes 589828
Sparse Core Ops, SparseCore 0:
  14.0 25.9 reduce-scatter.2
  64.7 21.5 all-reduce.5
  93.6 23.3 reduce-scatter.4
  142.0 288.0 all-reduce.9
  432.8 22.3 all-reduce.7
where the time goes:
time: 464 us; the launch traced here: 463 us
  waiting for transfers between devices  334 us (72%)
  blocking collectives  45.5 us (10%)
  matrix products  37.2 us (8%)
  local copies, waits for them, and re-layouts  16.4 us (4%)
  other arithmetic  14.9 us (3%)
  between operations  14.5 us (3%)
    psum x1, waiting for transfers between devices, shards(): grad_up = lax.psum(up_part.astype(jnp.bfloat16), 'ctx').astype(jnp.float32)  268 us
    all_gather x2, blocking collectives, collect(): return lax.all_gather(row_block, 'row', axis=0, tiled=True)  35.9 us
    reduce_scatter x1, waiting for transfers between devices, shards(): lax.psum_scatter(jnp.dot(context, up_weight, preferred_element_type=jnp.f...  26.1 us
    dot_general x4, matrix products, contract(): lax.dot_general(left_side, right_side, (((left_dim,), (right_dim,)), ((),...  25.9 us
    psum x2, waiting for transfers between devices, feature_total(): lax.psum(partial_terms.astype(jnp.bfloat16), 'col').astype(jnp.float32)  22.6 us
    reduce_scatter x1, waiting for transfers between devices, shards(): lax.psum_scatter(back_terms.astype(jnp.bfloat16), 'row', scatter_dimensio...  17.6 us
    unnamed x18, local copies, waits for them, and re-layouts  16.4 us
    convert_element_type x1, other arithmetic, shards(): lax.psum(down_part.astype(jnp.bfloat16), 'ctx').astype(jnp.float32)  11.8 us
  transfers between devices with their start and end apart: 5, of which 5 were waited for; matrix products, arithmetic and copies ran while one was open for 8% of the time, Pallas kernels for 0%

commit v1 on v0

--- a/solution.py
+++ b/solution.py
@@ -1,7 +1,30 @@
+import functools
 import jax
 import jax.numpy as jnp
 from jax import lax
 from jax.sharding import PartitionSpec as P
+
+
+def extend_target(here_x, along_axis):
+    axis_len = lax.axis_size(along_axis)
+    so_far_all = tuple(((kk, (kk + 1) % axis_len) for kk in range(axis_len)))
+    pages = tuple(((kk, (kk - 1) % axis_len) for kk in range(axis_len)))
+    latest, work_now = ([here_x], [here_x])
+    for _ in range(axis_len // 2):
+        latest.append(lax.ppermute(latest[-1], axis_name=along_axis, perm=so_far_all))
+    it = 0
+    while it < (axis_len - 1) // 2:
+        work_now.append(lax.ppermute(work_now[-1], axis_name=along_axis, perm=pages))
+        it = it + 1
+    state_now = jnp.roll(
+        jnp.concatenate([*latest[::-1], *work_now[1:]], 0),
+        (lax.axis_index(along_axis) - axis_len // 2) * here_x.shape[0],
+        axis=0,
+    )
+    return state_now
+
+
+fields_advance = functools.partial(extend_target, along_axis="row")
 
 
 def silu_slope(hidden):
@@ -10,7 +33,7 @@
 
 
 def collect(row_block):
-    return lax.all_gather(row_block, "row", axis=0, tiled=True)
+    return fields_advance(row_block)
 
 
 def feature_total(partial_terms):

time: 464 us -> 466 us (level)
  blocking collectives: 45.5 us -> 10.5 us
  waiting for transfers between devices: 334 us -> 359 us
  starting transfers between devices: 0.39 us -> 7.95 us
  other arithmetic: 14.9 us -> 19.9 us
    all_gather x2 -> x0, blocking collectives: 35.9 us -> none  [collect(): return lax.all_gather(row_block, 'row', axis=0, tiled=True)]
    ppermute x0 -> x6, waiting for transfers between devices: none -> 20.2 us  [the longest x4 19.3 us: extend_target(): lax.ppermute(latest[-1], axis_name=along_axis, perm=so_far_all)]
    ppermute x0 -> x6, starting transfers between devices: none -> 7.74 us  [the longest x2 7.62 us: extend_target(): lax.ppermute(work_now[-1], axis_name=along_axis, perm=pages)]
    reduce_scatter x1, waiting for transfers between devices: 17.6 us -> 23.4 us  [shards(): lax.psum_scatter(back_terms.astype(jnp.bfloat16), 'row', scatter_dimensio...]
    concatenate x0 -> x2, other arithmetic: none -> 5 us  [extend_target(): jnp.roll(jnp.concatenate([*latest[::-1], *work_now[1:]], 0), (lax.axis_in...]
  transfers between devices with their start and end apart: 5 -> 11, of which waited for: 5 -> 10; matrix products, arithmetic and copies ran while one was open for 8% -> 8% of each run, Pallas kernels for 0% -> 0%
where the time goes in v1:
time: 466 us; the launch traced here: 465 us
  waiting for transfers between devices  359 us (77%)
  matrix products  36.8 us (8%)
  other arithmetic  19.9 us (4%)
  local copies, waits for them, and re-layouts  16.6 us (4%)
  between operations  14.5 us (3%)
  blocking collectives  10.5 us (2%)
  starting transfers between devices  7.95 us (2%)
    psum x1, waiting for transfers between devices, shards(): grad_up = lax.psum(up_part.astype(jnp.bfloat16), 'ctx').astype(jnp.float32)  268 us
    reduce_scatter x1, waiting for transfers between devices, shards(): lax.psum_scatter(jnp.dot(context, up_weight, preferred_element_type=jnp.f...  26.1 us
    dot_general x4, matrix products, contract(): lax.dot_general(left_side, right_side, (((left_dim,), (right_dim,)), ((),...  25.5 us
    reduce_scatter x1, waiting for transfers between devices, shards(): lax.psum_scatter(back_terms.astype(jnp.bfloat16), 'row', scatter_dimensio...  23.4 us
    psum x2, waiting for transfers between devices, feature_total(): lax.psum(partial_terms.astype(jnp.bfloat16), 'col').astype(jnp.float32)  21.5 us
    ppermute x4, waiting for transfers between devices, extend_target(): lax.ppermute(latest[-1], axis_name=along_axis, perm=so_far_all)  19.3 us
    unnamed x18, local copies, waits for them, and re-layouts  16.6 us
    convert_element_type x1, other arithmetic, shards(): lax.psum(down_part.astype(jnp.bfloat16), 'ctx').astype(jnp.float32)  11.8 us
  transfers between devices with their start and end apart: 11, of which 10 were waited for; matrix products, arithmetic and copies ran while one was open for 8% of the time, Pallas kernels for 0%

profile of v1, /device:TPU:0, one launch (start us, length us, event | category | flops | bytes accessed | tf_op | source)
XLA Modules:
  0.0 465.5 jit_solution(10602310360964570282)
XLA Ops:
  8.1 5.7 %convolution_convert_fusion.2 = bf16[96,4096]{1,0:T(8,128)(2,1)} fusion(bf16[96,1024]{1,0:T(8,128)(2,1)S(1)} %copy-done, bf16[1024,4096]{1,0:T(8,128)(2,1)} %param.9), kind=kOutput, calls=%fused_computation.3 | convolution fusion | flops 805699584 | bytes 9371648 | tf_op jit(solution)/shard_map/dot_general | solution.py:54
  13.9 26.1 %reduce-scatter.3.cloned.1.call-done = bf16[24,4096]{1,0:T(8,128)(2,1)} async-done(((bf16[96,4096]{1,0:T(8,128)(2,1)}), bf16[24,4096]{1,0:T(8,128)(2,1)}) %reduce-scatter.3.cloned.1.call-update) | async-done | bytes 196624 | tf_op jit(solution)/shard_map/reduce_scatter | solution.py:53
  40.0 1.0 fusion.21
  41.1 3.8 collective-permute-start.2
  44.9 5.5 %collective-permute-done = bf16[24,4096]{1,0:T(8,128)(2,1)S(1)} collective-permute-done((bf16[24,4096]{1,0:T(8,128)(2,1)S(1)}, bf16[24,4096]{1,0:T(8,128)(2,1)S(1)}, u32[]{:S(2)}, u32[]{:S(2)}) %collective-permute-start) | collective-permute-done | bytes 196640 | tf_op jit(solution)/shard_map/ppermute | solution.py:14
  51.3 6.6 %collective-permute-done.1 = bf16[24,4096]{1,0:T(8,128)(2,1)S(1)} collective-permute-done((bf16[24,4096]{1,0:T(8,128)(2,1)S(1)}, bf16[24,4096]{1,0:T(8,128)(2,1)S(1)}, u32[]{:S(2)}, u32[]{:S(2)}) %collective-permute-start.1) | collective-permute-done | bytes 196640 | tf_op jit(solution)/shard_map/ppermute | solution.py:14
  57.9 2.5 fusion.10
  60.4 5.6 %convolution_convert_fusion.4 = bf16[96,1024]{1,0:T(8,128)(2,1)} fusion(bf16[96,4096]{1,0:T(8,128)(2,1)S(1)} %fusion.10, bf16[4096,1024]{1,0:T(8,128)(2,1)} %param.10), kind=kOutput, calls=%fused_computation.21 | convolution fusion | flops 805404672 | bytes 9371648 | tf_op jit(solution)/shard_map/dot_general | solution.py:60
  66.1 20.6 %all-reduce.6.cloned.1.call-done = bf16[96,1024]{1,0:T(8,128)(2,1)} async-done(((bf16[96,1024]{1,0:T(8,128)(2,1)}), bf16[96,1024]{1,0:T(8,128)(2,1)}) %all-reduce.6.cloned.1.call-update) | async-done | bytes 196624 | tf_op jit(solution)/shard_map/psum | solution.py:40
  86.7 7.1 %convolution_convert_fusion.1 = bf16[96,4096]{1,0:T(8,128)(2,1)} fusion(bf16[4096,1024]{1,0:T(8,128)(2,1)} %param.10, bf16[96,1024]{1,0:T(8,128)(2,1)S(1)} %copy-done.2, bf16[96,1024]{1,0:T(8,128)(2,1)} %all-reduce.6.cloned.1.call-done, bf16[96,1024]{1,0:T(8,128)(2,1)S(1)} %copy-done.3), kind=kOutput, calls=%fused_computation.2 | convolution fusion | flops 806780928 | bytes 9764864 | tf_op jit(solution)/shard_map/dot_general | solution.py:44
  93.9 23.4 %reduce-scatter.5.cloned.1.call-done = bf16[24,4096]{1,0:T(8,128)(2,1)} async-done(((bf16[96,4096]{1,0:T(8,128)(2,1)}), bf16[24,4096]{1,0:T(8,128)(2,1)}) %reduce-scatter.5.cloned.1.call-update) | async-done | bytes 196624 | tf_op jit(solution)/shard_map/reduce_scatter | solution.py:73
  117.3 1.1 fusion.25
  118.4 3.8 collective-permute-start.5
  122.2 5.5 %collective-permute-done.3 = bf16[24,4096]{1,0:T(8,128)(2,1)S(1)} collective-permute-done((bf16[24,4096]{1,0:T(8,128)(2,1)S(1)}, bf16[24,4096]{1,0:T(8,128)(2,1)S(1)}, u32[]{:S(2)}, u32[]{:S(2)}) %collective-permute-start.3) | collective-permute-done | bytes 196640 | tf_op jit(solution)/shard_map/ppermute | solution.py:14
  127.8 5.8 %convolution_convert_fusion = bf16[4096,1024]{1,0:T(8,128)(2,1)} fusion(bf16[96,4096]{1,0:T(8,128)(2,1)S(1)} %fusion.10, bf16[96,1024]{1,0:T(8,128)(2,1)S(1)} %copy-done.2, bf16[96,1024]{1,0:T(8,128)(2,1)S(1)} %copy-done.4, bf16[96,1024]{1,0:T(8,128)(2,1)S(1)} %copy-done.3), kind=kOutput, calls=%fused_computation.1 | convolution fusion | flops 810582016 | bytes 9764864 | tf_op jit(solution)/shard_map/dot_general | solution.py:44
  133.6 1.6 collective-permute-done.4
  135.2 2.5 fusion.3
  137.7 5.8 %convert_bitcast_fusion = bf16[1024,4096]{0,1:T(8,128)(2,1)} fusion(bf16[96,4096]{1,0:T(8,128)(2,1)S(1)} %fusion.3, bf16[96,1024]{1,0:T(8,128)(2,1)S(1)} %copy-done), kind=kOutput, calls=%fused_computation | convolution fusion | flops 809500672 | bytes 9371648 | tf_op jit(solution)/shard_map/dot_general | solution.py:44
  145.4 6.8 %convolution_convert_fusion.3 = bf16[96,1024]{1,0:T(8,128)(2,1)} fusion(bf16[96,4096]{1,0:T(8,128)(2,1)S(1)} %fusion.3, bf16[1024,4096]{1,0:T(8,128)(2,1)} %param.9), kind=kOutput, calls=%fused_computation.20 | convolution fusion | flops 805404672 | bytes 9371648 | tf_op jit(solution)/shard_map/dot_general | solution.py:44
  153.2 10.5 %all-reduce = f32[96]{0:T(128)S(1)} all-reduce(f32[96]{0:T(128)S(1)} %neg.13), channel_id=3, replica_groups=mesh['ctx'=4,'row'=4,'col'=2] {'row'}, use_global_device_ids=true, to_apply=%region_3.5.clone | all-reduce | flops 96 | bytes 768
  164.4 267.9 %all-reduce.10.cloned.1.call-done = (bf16[1024,4096]{0,1:T(8,128)(2,1)}, bf16[4096,1024]{1,0:T(8,128)(2,1)}) async-done(((bf16[1024,4096]{0,1:T(8,128)(2,1)}, bf16[4096,1024]{1,0:T(8,128)(2,1)}), (bf16[1024,4096]{0,1:T(8,128)(2,1)}, bf16[4096,1024]{1,0:T(8,128)(2,1)})) %all-reduce.10.cloned.1.call-update) | async-done | bytes 16777232 | tf_op jit(solution)/shard_map/psum | solution.py:83
  432.3 12.3 %copy.12 = f32[1024,4096]{1,0:T(8,128)} copy(bf16[1024,4096]{0,1:T(8,128)(2,1)} %get-tuple-element.19) | data formatting | bytes 25165824
  444.6 11.8 %convert_element_type.77 = f32[4096,1024]{1,0:T(8,128)} convert(bf16[4096,1024]{1,0:T(8,128)(2,1)} %get-tuple-element.20) | non-fusion elementwise | flops 4194304 | bytes 25165824 | tf_op jit(solution)/shard_map/convert_element_type | solution.py:71
  457.3 1.6 copy.17
  (35 shorter events, 5.9 us)
Async XLA Ops:
  7.2 0.9 copy-start
  7.2 32.8 %reduce-scatter.3.cloned.1.call-start = ((), (), s32[]{:S(2)}) async-start(), calls=%async_computation.2 | async-start | bytes 983040 | tf_op jit(solution)/shard_map/reduce_scatter | solution.py:53
  13.8 72.8 %all-reduce.6.cloned.1.call-start = ((), (), s32[]{:S(2)}) async-start(), calls=%async_computation.3 | async-start | bytes 393216 | tf_op jit(solution)/shard_map/psum | solution.py:40
  41.0 9.4 %collective-permute-start = (bf16[24,4096]{1,0:T(8,128)(2,1)S(1)}, bf16[24,4096]{1,0:T(8,128)(2,1)S(1)}, u32[]{:S(2)}, u32[]{:S(2)}) collective-permute-start(bf16[24,4096]{1,0:T(8,128)(2,1)S(1)} %fusion.21), channel_id=1, source_target_pairs={{0,2},{2,4},{4,6},{6,0},{1,3},{3,5},{5,7},{7,1},{8,10},{10,12},{12... | collective-permute-start | bytes 589832 | tf_op jit(solution)/shard_map/ppermute | solution.py:14
  41.1 10.2 %collective-permute-start.2 = (bf16[24,4096]{1,0:T(8,128)(2,1)S(1)}, bf16[24,4096]{1,0:T(8,128)(2,1)S(1)}, u32[]{:S(2)}, u32[]{:S(2)}) collective-permute-start(bf16[24,4096]{1,0:T(8,128)(2,1)S(1)} %fusion.21), channel_id=1, source_target_pairs={{0,6},{2,0},{4,2},{6,4},{1,7},{3,1},{5,3},{7,5},{8,14},{10,8},{12,... | collective-permute-start | bytes 589832 | tf_op jit(solution)/shard_map/ppermute | solution.py:17
  50.4 7.5 %collective-permute-start.1 = (bf16[24,4096]{1,0:T(8,128)(2,1)S(1)}, bf16[24,4096]{1,0:T(8,128)(2,1)S(1)}, u32[]{:S(2)}, u32[]{:S(2)}) collective-permute-start(bf16[24,4096]{1,0:T(8,128)(2,1)S(1)} %collective-permute-done), channel_id=1, source_target_pairs={{0,2},{2,4},{4,6},{6,0},{1,3},{3,5},{5,7},{7,1},{8,10},{10,12},{12... | collective-permute-start | bytes 589832 | tf_op jit(solution)/shard_map/ppermute | solution.py:14
  60.4 26.2 %copy-start.2 = (bf16[96,1024]{1,0:T(8,128)(2,1)S(1)}, bf16[96,1024]{1,0:T(8,128)(2,1)}, u32[]{:S(2)}) copy-start(bf16[96,1024]{1,0:T(8,128)(2,1)} %param.11) | copy-start | bytes 589828
  60.4 26.2 %copy-start.3 = (bf16[96,1024]{1,0:T(8,128)(2,1)S(1)}, bf16[96,1024]{1,0:T(8,128)(2,1)}, u32[]{:S(2)}) copy-start(bf16[96,1024]{1,0:T(8,128)(2,1)} %param.7) | copy-start | bytes 589828
  66.0 51.2 %copy-start.5 = (bf16[24,4096]{1,0:T(8,128)(2,1)S(1)}, bf16[24,4096]{1,0:T(8,128)(2,1)}, u32[]{:S(2)}) copy-start(bf16[24,4096]{1,0:T(8,128)(2,1)} %reduce-scatter.3.cloned.1.call-done) | copy-start | bytes 589828
  66.0 51.2 %reduce-scatter.5.cloned.1.call-start = ((), (), s32[]{:S(2)}) async-start(), calls=%async_computation.4 | async-start | bytes 983040 | tf_op jit(solution)/shard_map/reduce_scatter | solution.py:73
  86.7 41.1 %copy-start.4 = (bf16[96,1024]{1,0:T(8,128)(2,1)S(1)}, bf16[96,1024]{1,0:T(8,128)(2,1)}, u32[]{:S(2)}) copy-start(bf16[96,1024]{1,0:T(8,128)(2,1)} %all-reduce.6.cloned.1.call-done) | copy-start | bytes 589828
  93.8 338.5 %all-reduce.10.cloned.1.call-start = ((), (), s32[]{:S(2)}) async-start(), calls=%async_computation.6 | async-start | bytes 33554432 | tf_op jit(solution)/shard_map/psum | solution.py:83
  118.4 9.4 %collective-permute-start.3 = (bf16[24,4096]{1,0:T(8,128)(2,1)S(1)}, bf16[24,4096]{1,0:T(8,128)(2,1)S(1)}, u32[]{:S(2)}, u32[]{:S(2)}) collective-permute-start(bf16[24,4096]{1,0:T(8,128)(2,1)S(1)} %fusion.25), channel_id=1, source_target_pairs={{0,2},{2,4},{4,6},{6,0},{1,3},{3,5},{5,7},{7,1},{8,10},{10,12},{12... | collective-permute-start | bytes 589832 | tf_op jit(solution)/shard_map/ppermute | solution.py:14
  118.4 15.2 %collective-permute-start.5 = (bf16[24,4096]{1,0:T(8,128)(2,1)S(1)}, bf16[24,4096]{1,0:T(8,128)(2,1)S(1)}, u32[]{:S(2)}, u32[]{:S(2)}) collective-permute-start(bf16[24,4096]{1,0:T(8,128)(2,1)S(1)} %fusion.25), channel_id=1, source_target_pairs={{0,6},{2,0},{4,2},{6,4},{1,7},{3,1},{5,3},{7,5},{8,14},{10,8},{12,... | collective-permute-start | bytes 589832 | tf_op jit(solution)/shard_map/ppermute | solution.py:17
  127.8 7.5 %collective-permute-start.4 = (bf16[24,4096]{1,0:T(8,128)(2,1)S(1)}, bf16[24,4096]{1,0:T(8,128)(2,1)S(1)}, u32[]{:S(2)}, u32[]{:S(2)}) collective-permute-start(bf16[24,4096]{1,0:T(8,128)(2,1)S(1)} %collective-permute-done.3), channel_id=1, source_target_pairs={{0,2},{2,4},{4,6},{6,0},{1,3},{3,5},{5,7},{7,1},{8,10},{10,12},{12... | collective-permute-start | bytes 589832 | tf_op jit(solution)/shard_map/ppermute | solution.py:14
  143.5 0.7 copy-start.6
  143.5 313.8 %all-reduce.8.cloned.1.call-start = ((), (), s32[]{:S(2)}) async-start(), calls=%async_computation.5 | async-start | bytes 393216 | tf_op jit(solution)/shard_map/psum | solution.py:40
  444.6 14.3 %copy-start.1 = (bf16[96,1024]{1,0:T(8,128)(2,1)S(1)}, bf16[96,1024]{1,0:T(8,128)(2,1)}, u32[]{:S(2)}) copy-start(bf16[96,1024]{1,0:T(8,128)(2,1)} %param.8) | copy-start | bytes 589828
Sparse Core Ops, SparseCore 0:
  14.0 25.9 reduce-scatter.2
  66.2 20.4 all-reduce.5
  93.9 23.2 reduce-scatter.4
  143.7 288.5 all-reduce.9
  435.0 22.3 all-reduce.7
